TPU v7x, 32 devices: a whole 2x2x4 slice. The times are simulated.
32 devices in a mesh: parts: 2 (over y), track: 4 (over z), tm: 2 (over x), coef: 2 (over core).
Axes of the slice: x: 2, y: 2, z: 4, core: 2. Of those that a mesh axis runs over, the one named last changes fastest.
Arguments:
- sector_ids: int32 [12288], P(('parts', 'track', 'tm')), parts along dimension 0, may hold values from 0 to 63, as said below
- observed: float32 [3, 12288], P(None, ('parts', 'track', 'tm')), parts along dimension 1, may hold values from -6 to 6
- weights: float32 [3, 12288], P(None, ('parts', 'track', 'tm')), parts along dimension 1, may hold values from 0.3 to 3
- coefficients: float32 [2048, 128], P(('parts', 'track')), parts along dimension 0, may hold values from -6 to 6
- tile_index: int32 [128, 12], P(('parts', 'track', 'tm'), 'coef'), parts along dimension 0, may hold values from 0 to 1023, as said below
- tile_count: int32 [128], P(('parts', 'track', 'tm')), parts along dimension 0, may hold values from 3 to 12
- sensitivity: bfloat16 [128, 12, 3, 128, 128], P(('parts', 'track', 'tm'), 'coef'), parts along dimension 0, may hold values from -0.15625 to 0.15625
Outputs:
- gradient: float32 [2048, 128], P(('parts', 'track')), parts along dimension 0
There are 2 independent parts, one for each index of `parts`. A program takes and returns all parts, laid end to end along the dimension named above; each array names one. Nothing has to cross between parts.
Inputs may be any that keep to these rules, and one draw needn't show every extreme that they name: `sector_ids`: the rows of one index of track and tm fall in at most 192 rows into the 8 consecutive sectors of any one index, and some pair reaches 192; the sectors of each index receive exactly 768 rows in all; each sector holds at most 128 rows, and every index holds a sector with exactly 128. `tile_index`: entries at positions from tile_count on are arbitrary blocks and take no part. Block n belongs to track index n // 256. Of the 48 entries held by one index of track, tm and coef (its sectors' rows, its coef share of the columns), live or not, at most 24 name blocks of any one track index, and every such device has a track index named exactly 24 times.
All inputs are finite; a program needn't handle non-finite values.
Results may differ from a plain program's by a relative error of at most 0.0037.
Values may be sent and summed in bfloat16 or wider, within the bound.
A program may use at most 64 MiB of HBM per device.

v0:
```python
import jax
import jax.numpy as jnp
from jax import lax
from jax.sharding import PartitionSpec as P

HUBER = 2.0


def per_device(sector_ids, observed, weights, coefficients, tile_index, tile_count, sensitivity):
    sector_total = tile_index.shape[0]
    half_k = tile_index.shape[1]
    slot_count = sensitivity.shape[3]
    block_width = sensitivity.shape[4]
    owners = lax.axis_size(("track", "tm"))
    row_total = sector_ids.shape[0]
    capacity = 2 * row_total // owners
    rounded = coefficients.astype(jnp.bfloat16)
    every_block = lax.all_gather(rounded, "track", axis=0, tiled=True)
    owner_of = sector_ids // sector_total
    local_sector = sector_ids % sector_total
    onehot = (owner_of[:, None] == jnp.arange(owners, dtype=jnp.int32)[None, :]).astype(jnp.int32)
    ranking = jnp.sum((jnp.cumsum(onehot, axis=0) - 1) * onehot, axis=1)
    placing = owner_of * capacity + ranking
    payload = jnp.concatenate([observed, weights], axis=0)
    outgoing = jnp.zeros((6, owners * capacity), jnp.float32).at[:, placing].set(payload)
    outgoing = jnp.transpose(outgoing.reshape(6, owners, capacity), (1, 0, 2))
    labels = jnp.full((owners * capacity,), -1, jnp.int32).at[placing].set(local_sector)
    labels = labels.reshape(owners, capacity)
    got_rows, got_labels = (
        lax.all_to_all(outgoing, ("track", "tm"), split_axis=0, concat_axis=0, tiled=True),
        lax.all_to_all(labels, ("track", "tm"), split_axis=0, concat_axis=0, tiled=True),
    )
    received = jnp.transpose(got_rows, (1, 0, 2)).reshape(6, owners * capacity)
    flat_labels = got_labels.reshape(owners * capacity)
    member = (flat_labels[:, None] == jnp.arange(sector_total, dtype=jnp.int32)[None, :]).astype(
        jnp.int32
    )
    within = jnp.sum((jnp.cumsum(member, axis=0) - 1) * member, axis=1)
    target = jnp.where(
        flat_labels >= 0, flat_labels * slot_count + within, sector_total * slot_count
    )
    gridded = jnp.zeros((6, sector_total * slot_count + 1), jnp.float32).at[:, target].set(received)
    gridded = jnp.transpose(gridded[:, :-1].reshape(6, sector_total, slot_count), (1, 0, 2))
    observed_tiles = gridded[:, :3]
    weight_tiles = gridded[:, 3:]
    k_global = lax.axis_index("coef") * half_k + jnp.arange(half_k, dtype=jnp.int32)
    active = k_global[None, :] < tile_count[:, None]
    blocks = jnp.take(every_block, tile_index, axis=0)
    blocks = jnp.where(active[:, :, None], blocks, jnp.zeros_like(blocks))
    partial_pred = jnp.einsum(
        "skcjb,skb->scj", sensitivity, blocks, preferred_element_type=jnp.float32
    )
    predicted = lax.psum(partial_pred, "coef")
    scaled = weight_tiles * (predicted - observed_tiles)
    force = (weight_tiles * scaled / jnp.sqrt(1.0 + (scaled / HUBER) ** 2)).astype(jnp.bfloat16)
    tile_grad = jnp.einsum("skcjb,scj->skb", sensitivity, force, preferred_element_type=jnp.float32)
    tile_grad = jnp.where(active[:, :, None], tile_grad, jnp.zeros_like(tile_grad))
    block_total = every_block.shape[0]
    partial_grad = jnp.zeros((block_total, block_width), jnp.float32)
    partial_grad = partial_grad.at[tile_index.reshape(-1)].add(tile_grad.reshape(-1, block_width))
    summed = lax.psum_scatter(partial_grad, "track", scatter_dimension=0, tiled=True)
    gradient = lax.psum(summed, ("tm", "coef"))
    return gradient


def solution(mesh):
    placed = (
        P(("parts", "track", "tm")),
        P(None, ("parts", "track", "tm")),
        P(None, ("parts", "track", "tm")),
        P(("parts", "track"), None),
        P(("parts", "track", "tm"), "coef"),
        P(("parts", "track", "tm")),
        P(("parts", "track", "tm"), "coef", None, None, None),
    )
    return jax.shard_map(
        per_device,
        mesh=mesh,
        in_specs=placed,
        out_specs=P(("parts", "track"), None),
        check_vma=False,
    )
```

profile of v0, /device:TPU:0, one launch (start us, length us, event | category | flops | bytes accessed | tf_op | source)
XLA Modules:
  0.0 135.0 jit_solution(9949122944024813271)
XLA Ops:
  6.5 0.7 add_select_fusion
  7.2 1.7 %reduce-window.14 = s32[8,6,128]{2,0,1:T(8,128)S(1)} reduce-window(s32[8,6,128]{2,0,1:T(8,128)S(1)} %fusion.13, s32[]{:T(128)} %constant.40.clone.1), window={size=1x1x128 pad=0_0x0_0x127_0}, to_apply=%region_0.1 | reduce-window | flops 780288 | bytes 49156 | tf_op jit(solution)/shard_map/reduce-window
  8.9 0.1 slice.30
  9.0 0.1 copy.24
  9.2 0.2 reduce-window.15
  9.3 0.1 copy.25
  9.4 0.1 fusion.11
  9.5 3.4 %scatter_custom_fusion = s32[1536]{0:T(1024)S(1)} fusion(s32[768]{0:T(1024)S(1)} %compare_select_fusion.2, s32[768]{0:T(1024)S(1)} %get-tuple-element.7, s32[]{:T(128)} %constant.74.clone.1), kind=kCustom, calls=%fused_computation.50 | custom fusion | bytes 6148 | tf_op jit(solution)/shard_map/scatter | solution.py:27
  12.9 0.7 all_to_all.9
  13.6 7.3 %all-to-all-start = ((s32[8,1,192]{2,1,0:T(1,128)}), s32[8,1,192]{2,1,0:T(1,128)S(1)}, u32[]{:S(2)}, u32[]{:S(2)}) async-start(s32[8,1,192]{2,1,0:T(1,128)} %all_to_all.9), calls=%async_computation | async-start | bytes 16384 | tf_op jit(solution)/shard_map/all_to_all | solution.py:31
  20.8 0.7 compare_select_fusion.1
  21.5 0.8 reshape.166
  22.3 0.7 maximum_bitcast_fusion
  23.0 0.2 copy.26
  23.2 4.4 %scatter_custom_fusion.1 = f32[6,1536]{0,1:T(8,128)S(1)} fusion(s32[768]{0:T(1024)S(1)} %compare_select_fusion.2, f32[768,6]{1,0:T(8,128)S(1)} %copy.26, f32[]{:T(128)} %constant.39.clone.1), kind=kCustom, calls=%fused_computation.7 | custom fusion | bytes 36868 | tf_op jit(solution)/shard_map/scatter | solution.py:25
  27.6 1.0 copy.27
  28.6 0.9 convert_element_type.18
  29.5 14.5 %all_gather.3 = bf16[1024,128]{1,0:T(8,128)(2,1)S(1)} all-gather(bf16[256,128]{1,0:T(8,128)(2,1)S(1)} %convert_element_type.18), channel_id=1, replica_groups=mesh['parts'=2,'track'=4,'tm'=2,'coef'=2] {'track'}, dimensions={0}, use_global_device_ids=true | all-gather | bytes 327680 | tf_op jit(solution)/shard_map/all_gather | solution.py:18
  44.0 0.1 reshape.175
  44.0 0.6 gather_fusion
  44.7 0.8 compare_and_fusion
  45.4 0.1 select_bitcast_fusion
  45.5 3.7 %fusion = f32[8,1,3,128,1]{3,1,4,2,0:T(1,128)S(1)} fusion(bf16[8,6,3,128,128]{4,3,2,1,0:T(8,128)(2,1)} %param.13, bf16[8,6,128,1,1]{2,1,0,3,4:T(8,128)(2,1)S(1)} %select_bitcast_fusion), kind=kOutput, calls=%fused_computation.5 | convolution fusion | flops 4718592 | bytes 4743168 | tf_op jit(solution)/shard_map/skcjb,skb->scj/dot_general | solution.py:50
  49.2 3.3 %psum.14 = f32[8,3,128]{2,0,1:T(8,128)S(1)} all-reduce(f32[8,3,128]{2,0,1:T(8,128)S(1)} %bitcast.50), channel_id=1, replica_groups=mesh['parts'=2,'track'=4,'tm'=2,'coef'=2] {'coef'}, use_global_device_ids=true, to_apply=%region_9.10 | all-reduce | flops 3072 | bytes 24576 | tf_op jit(solution)/shard_map/psum | solution.py:53
  52.5 0.0 all-to-all-done
  52.5 5.7 %all-to-all-start.1 = ((f32[8,6,192]{2,1,0:T(8,128)}), f32[8,6,192]{2,1,0:T(8,128)S(1)}, u32[]{:S(2)}, u32[]{:S(2)}) async-start(f32[8,6,192]{2,1,0:T(8,128)} %bitcast.8), calls=%async_computation.1 | async-start | bytes 131072 | tf_op jit(solution)/shard_map/all_to_all | solution.py:30
  58.2 0.0 reduce-scatter.2.cloned.1.call-start
  58.3 0.1 eq.61
  58.4 0.1 eq.57
  58.5 2.3 %reduce-window.16 = s32[8,12,128]{2,1,0:T(8,128)S(1)} reduce-window(s32[8,12,128]{2,1,0:T(8,128)S(1)} %fusion.8, s32[]{:T(128)} %constant.40.clone.1), window={size=1x1x128 pad=0_0x0_0x127_0}, to_apply=%region_4.5 | reduce-window | flops 1560576 | bytes 98308 | tf_op jit(solution)/shard_map/reduce-window.2
  60.7 0.3 slice_reduce_fusion
  61.0 0.2 reduce-window.19
  61.2 0.1 add_bitcast_fusion
  61.3 0.1 mul.43
  61.4 0.1 ge.21
  61.6 3.5 %all-to-all-done.1 = f32[8,6,192]{2,1,0:T(8,128)S(1)} async-done(((f32[8,6,192]{2,1,0:T(8,128)}), f32[8,6,192]{2,1,0:T(8,128)S(1)}, u32[]{:S(2)}, u32[]{:S(2)}) %all-to-all-start.1) | async-done | bytes 36896 | tf_op jit(solution)/shard_map/all_to_all | solution.py:30
  65.1 0.1 reshape.198
  65.2 0.3 copy.29
  65.5 4.4 %scatter_custom_fusion.2 = f32[6,1025]{0,1:T(8,128)S(1)} fusion(s32[1536]{0:T(1024)S(1)} %fusion.17, f32[1536,6]{1,0:T(8,128)S(1)} %copy.29, f32[]{:T(128)} %constant.39.clone.1), kind=kCustom, calls=%fused_computation.9 | custom fusion | bytes 24604 | tf_op jit(solution)/shard_map/scatter | solution.py:42
  70.0 0.2 copy.36
  70.2 3.1 %fusion.15 = f32[8,1,6,128,1]{3,1,4,2,0:T(1,128)S(1)} fusion(bf16[8,6,3,128,128]{4,3,2,1,0:T(8,128)(2,1)} %param.13, bf16[8,3,128,1,1]{2,0,1,3,4:T(8,128)(2,1)S(1)} %fusion.18), kind=kOutput, calls=%fused_computation.34 | convolution fusion | flops 4718592 | bytes 4749312 | tf_op jit(solution)/shard_map/skcjb,scj->skb/dot_general | solution.py:56
  73.3 0.1 bitcast_select_fusion
  73.4 1.5 %scatter_custom_fusion.3 = f32[1024,128]{1,0:T(8,128)} fusion(s32[48]{0:T(128)S(1)} %fusion.23, f32[48,128]{1,0:T(8,128)S(1)} %reshape.209, f32[]{:T(128)} %constant.39.clone.1), kind=kCustom, calls=%fused_computation.11 | custom fusion | flops 6144 | bytes 524292 | tf_op jit(solution)/shard_map/scatter-add | solution.py:60
  74.9 0.0 reduce-scatter.2.cloned.1.call-update
  75.0 0.0 all-reduce.2.cloned.1.call-start
  75.0 19.6 %reduce-scatter.2.cloned.1.call-done = f32[256,128]{1,0:T(8,128)} async-done(((f32[1024,128]{1,0:T(8,128)}), f32[256,128]{1,0:T(8,128)}) %reduce-scatter.2.cloned.1.call-update) | async-done | bytes 131088 | tf_op jit(solution)/shard_map/reduce_scatter | solution.py:61
  94.6 0.0 all-reduce.2.cloned.1.call-update
  94.7 32.0 %all-reduce.2.cloned.1.call-done = f32[256,128]{1,0:T(8,128)} async-done(((f32[256,128]{1,0:T(8,128)}), f32[256,128]{1,0:T(8,128)}) %all-reduce.2.cloned.1.call-update) | async-done | bytes 131088 | tf_op jit(solution)/shard_map/psum | solution.py:62
  126.6 1.6 %copy.49 = f32[256,128]{1,0:T(8,128)} copy(f32[256,128]{1,0:T(8,128)} %all-reduce.2.cloned.1.call-done) | data formatting | bytes 262144
  (16 shorter events, 0.3 us)
Async XLA Ops:
  13.6 38.9 %all-to-all-start = ((s32[8,1,192]{2,1,0:T(1,128)}), s32[8,1,192]{2,1,0:T(1,128)S(1)}, u32[]{:S(2)}, u32[]{:S(2)}) async-start(s32[8,1,192]{2,1,0:T(1,128)} %all_to_all.9), calls=%async_computation | async-start | bytes 16384 | tf_op jit(solution)/shard_map/all_to_all | solution.py:31
  52.5 12.6 %all-to-all-start.1 = ((f32[8,6,192]{2,1,0:T(8,128)}), f32[8,6,192]{2,1,0:T(8,128)S(1)}, u32[]{:S(2)}, u32[]{:S(2)}) async-start(f32[8,6,192]{2,1,0:T(8,128)} %bitcast.8), calls=%async_computation.1 | async-start | bytes 131072 | tf_op jit(solution)/shard_map/all_to_all | solution.py:30
  58.2 36.4 %reduce-scatter.2.cloned.1.call-start = ((), (), s32[]{:S(2)}) async-start(), calls=%async_computation.3 | async-start | bytes 655360 | tf_op jit(solution)/shard_map/reduce_scatter | solution.py:61
  75.0 51.7 %all-reduce.2.cloned.1.call-start = ((), (), s32[]{:S(2)}) async-start(), calls=%async_computation.4 | async-start | bytes 262144 | tf_op jit(solution)/shard_map/psum | solution.py:62
Sparse Core Ops, SparseCore 0:
  75.1 19.5 reduce-scatter.1
  97.0 29.6 all-reduce.1
where the time goes:
time: 136 us; the launch traced here: 135 us
  waiting for transfers between devices  55.2 us (41%)
  local copies, waits for them, and re-layouts  18.6 us (14%)
  blocking collectives  17.8 us (13%)
  between operations  13.5 us (10%)
  starting transfers between devices  13.1 us (10%)
  other arithmetic  10.2 us (7%)
  matrix products  6.73 us (5%)
    psum x1, waiting for transfers between devices, per_device(): gradient = lax.psum(summed, ('tm', 'coef'))  32 us
    reduce_scatter x1, waiting for transfers between devices, per_device(): lax.psum_scatter(partial_grad, 'track', scatter_dimension=0, tiled=True)  19.6 us
    all_gather x1, blocking collectives, per_device(): every_block = lax.all_gather(rounded, 'track', axis=0, tiled=True)  14.5 us
    all_to_all x1, starting transfers between devices, per_device(): lax.all_to_all(labels, ('track', 'tm'), split_axis=0, concat_axis=0, tile...  7.25 us
    all_to_all x1, starting transfers between devices, per_device(): lax.all_to_all(outgoing, ('track', 'tm'), split_axis=0, concat_axis=0, ti...  5.72 us
    scatter x1, local copies, waits for them, and re-layouts, per_device(): jnp.zeros((6, sector_total * slot_count + 1), jnp.float32).at[:, target]  4.45 us
    scatter x1, local copies, waits for them, and re-layouts, per_device(): jnp.zeros((6, owners * capacity), jnp.float32).at[:, placing].set(payload)  4.36 us
    another operation x4, other arithmetic  4.31 us
  transfers between devices with their start and end apart: 4, of which 3 were waited for; matrix products, arithmetic and copies ran while one was open for 13% of the time, Pallas kernels for 0%

commit v1 on v0

--- a/solution.py
+++ b/solution.py
@@ -59,7 +59,7 @@
     partial_grad = jnp.zeros((block_total, block_width), jnp.float32)
     partial_grad = partial_grad.at[tile_index.reshape(-1)].add(tile_grad.reshape(-1, block_width))
     summed = lax.psum_scatter(partial_grad, "track", scatter_dimension=0, tiled=True)
-    gradient = lax.psum(summed, ("tm", "coef"))
+    gradient = lax.psum(lax.psum(summed, "coef"), "tm")
     return gradient
 
 

time: 136 us -> 147 us (1.081)
  waiting for transfers between devices: 55.2 us -> 66.5 us
    psum x1 -> x2, waiting for transfers between devices: 32 us -> 43.3 us  [per_device(): gradient = lax.psum(lax.psum(summed, 'coef'), 'tm')]
  transfers between devices with their start and end apart: 4 -> 5, of which waited for: 3 -> 4; matrix products, arithmetic and copies ran while one was open for 13% -> 12% of each run, Pallas kernels for 0% -> 0%
where the time goes in v1:
time: 147 us; the launch traced here: 146 us
  waiting for transfers between devices  66.5 us (45%)
  local copies, waits for them, and re-layouts  18.6 us (13%)
  blocking collectives  17.8 us (12%)
  between operations  13.3 us (9%)
  starting transfers between devices  13.1 us (9%)
  other arithmetic  10.2 us (7%)
  matrix products  6.73 us (5%)
    psum x2, waiting for transfers between devices, per_device(): gradient = lax.psum(lax.psum(summed, 'coef'), 'tm')  43.3 us
    reduce_scatter x1, waiting for transfers between devices, per_device(): lax.psum_scatter(partial_grad, 'track', scatter_dimension=0, tiled=True)  19.6 us
    all_gather x1, blocking collectives, per_device(): every_block = lax.all_gather(rounded, 'track', axis=0, tiled=True)  14.5 us
    all_to_all x1, starting transfers between devices, per_device(): lax.all_to_all(labels, ('track', 'tm'), split_axis=0, concat_axis=0, tile...  7.25 us
    all_to_all x1, starting transfers between devices, per_device(): lax.all_to_all(outgoing, ('track', 'tm'), split_axis=0, concat_axis=0, ti...  5.72 us
    scatter x1, local copies, waits for them, and re-layouts, per_device(): jnp.zeros((6, sector_total * slot_count + 1), jnp.float32).at[:, target]  4.45 us
    scatter x1, local copies, waits for them, and re-layouts, per_device(): jnp.zeros((6, owners * capacity), jnp.float32).at[:, placing].set(payload)  4.36 us
    another operation x4, other arithmetic  4.31 us
  transfers between devices with their start and end apart: 5, of which 4 were waited for; matrix products, arithmetic and copies ran while one was open for 12% of the time, Pallas kernels for 0%

profile of v1, /device:TPU:0, one launch (start us, length us, event | category | flops | bytes accessed | tf_op | source)
XLA Modules:
  0.0 146.1 jit_solution(9573276944461057414)
XLA Ops:
  6.5 0.7 add_select_fusion
  7.2 1.7 %reduce-window.14 = s32[8,6,128]{2,0,1:T(8,128)S(1)} reduce-window(s32[8,6,128]{2,0,1:T(8,128)S(1)} %fusion.13, s32[]{:T(128)} %constant.40.clone.1), window={size=1x1x128 pad=0_0x0_0x127_0}, to_apply=%region_0.1 | reduce-window | flops 780288 | bytes 49156 | tf_op jit(solution)/shard_map/reduce-window
  8.9 0.1 slice.30
  9.0 0.1 copy.24
  9.2 0.2 reduce-window.15
  9.3 0.1 copy.25
  9.4 0.1 fusion.11
  9.5 3.4 %scatter_custom_fusion = s32[1536]{0:T(1024)S(1)} fusion(s32[768]{0:T(1024)S(1)} %compare_select_fusion.2, s32[768]{0:T(1024)S(1)} %get-tuple-element.7, s32[]{:T(128)} %constant.74.clone.1), kind=kCustom, calls=%fused_computation.50 | custom fusion | bytes 6148 | tf_op jit(solution)/shard_map/scatter | solution.py:27
  12.9 0.7 all_to_all.9
  13.6 7.3 %all-to-all-start = ((s32[8,1,192]{2,1,0:T(1,128)}), s32[8,1,192]{2,1,0:T(1,128)S(1)}, u32[]{:S(2)}, u32[]{:S(2)}) async-start(s32[8,1,192]{2,1,0:T(1,128)} %all_to_all.9), calls=%async_computation | async-start | bytes 16384 | tf_op jit(solution)/shard_map/all_to_all | solution.py:31
  20.8 0.7 compare_select_fusion.1
  21.5 0.8 reshape.166
  22.3 0.7 maximum_bitcast_fusion
  23.0 0.2 copy.26
  23.2 4.4 %scatter_custom_fusion.1 = f32[6,1536]{0,1:T(8,128)S(1)} fusion(s32[768]{0:T(1024)S(1)} %compare_select_fusion.2, f32[768,6]{1,0:T(8,128)S(1)} %copy.26, f32[]{:T(128)} %constant.39.clone.1), kind=kCustom, calls=%fused_computation.7 | custom fusion | bytes 36868 | tf_op jit(solution)/shard_map/scatter | solution.py:25
  27.6 1.0 copy.27
  28.6 0.9 convert_element_type.18
  29.5 14.5 %all_gather.3 = bf16[1024,128]{1,0:T(8,128)(2,1)S(1)} all-gather(bf16[256,128]{1,0:T(8,128)(2,1)S(1)} %convert_element_type.18), channel_id=1, replica_groups=mesh['parts'=2,'track'=4,'tm'=2,'coef'=2] {'track'}, dimensions={0}, use_global_device_ids=true | all-gather | bytes 327680 | tf_op jit(solution)/shard_map/all_gather | solution.py:18
  44.0 0.1 reshape.175
  44.0 0.6 gather_fusion
  44.7 0.8 compare_and_fusion
  45.4 0.1 select_bitcast_fusion
  45.5 3.7 %fusion = f32[8,1,3,128,1]{3,1,4,2,0:T(1,128)S(1)} fusion(bf16[8,6,3,128,128]{4,3,2,1,0:T(8,128)(2,1)} %param.13, bf16[8,6,128,1,1]{2,1,0,3,4:T(8,128)(2,1)S(1)} %select_bitcast_fusion), kind=kOutput, calls=%fused_computation.5 | convolution fusion | flops 4718592 | bytes 4743168 | tf_op jit(solution)/shard_map/skcjb,skb->scj/dot_general | solution.py:50
  49.2 3.3 %psum.21 = f32[8,3,128]{2,0,1:T(8,128)S(1)} all-reduce(f32[8,3,128]{2,0,1:T(8,128)S(1)} %bitcast.50), channel_id=1, replica_groups=mesh['parts'=2,'track'=4,'tm'=2,'coef'=2] {'coef'}, use_global_device_ids=true, to_apply=%region_9.10 | all-reduce | flops 3072 | bytes 24576 | tf_op jit(solution)/shard_map/psum | solution.py:53
  52.5 0.0 all-to-all-done
  52.5 5.7 %all-to-all-start.1 = ((f32[8,6,192]{2,1,0:T(8,128)}), f32[8,6,192]{2,1,0:T(8,128)S(1)}, u32[]{:S(2)}, u32[]{:S(2)}) async-start(f32[8,6,192]{2,1,0:T(8,128)} %bitcast.8), calls=%async_computation.1 | async-start | bytes 131072 | tf_op jit(solution)/shard_map/all_to_all | solution.py:30
  58.2 0.0 reduce-scatter.2.cloned.1.call-start
  58.3 0.1 eq.61
  58.4 0.1 eq.57
  58.5 2.3 %reduce-window.16 = s32[8,12,128]{2,1,0:T(8,128)S(1)} reduce-window(s32[8,12,128]{2,1,0:T(8,128)S(1)} %fusion.8, s32[]{:T(128)} %constant.40.clone.1), window={size=1x1x128 pad=0_0x0_0x127_0}, to_apply=%region_4.5 | reduce-window | flops 1560576 | bytes 98308 | tf_op jit(solution)/shard_map/reduce-window.2
  60.7 0.3 slice_reduce_fusion
  61.0 0.2 reduce-window.19
  61.2 0.1 add_bitcast_fusion
  61.3 0.1 mul.43
  61.4 0.1 ge.21
  61.6 3.5 %all-to-all-done.1 = f32[8,6,192]{2,1,0:T(8,128)S(1)} async-done(((f32[8,6,192]{2,1,0:T(8,128)}), f32[8,6,192]{2,1,0:T(8,128)S(1)}, u32[]{:S(2)}, u32[]{:S(2)}) %all-to-all-start.1) | async-done | bytes 36896 | tf_op jit(solution)/shard_map/all_to_all | solution.py:30
  65.1 0.1 reshape.198
  65.2 0.3 copy.29
  65.5 4.4 %scatter_custom_fusion.2 = f32[6,1025]{0,1:T(8,128)S(1)} fusion(s32[1536]{0:T(1024)S(1)} %fusion.17, f32[1536,6]{1,0:T(8,128)S(1)} %copy.29, f32[]{:T(128)} %constant.39.clone.1), kind=kCustom, calls=%fused_computation.9 | custom fusion | bytes 24604 | tf_op jit(solution)/shard_map/scatter | solution.py:42
  70.0 0.2 copy.36
  70.2 3.1 %fusion.15 = f32[8,1,6,128,1]{3,1,4,2,0:T(1,128)S(1)} fusion(bf16[8,6,3,128,128]{4,3,2,1,0:T(8,128)(2,1)} %param.13, bf16[8,3,128,1,1]{2,0,1,3,4:T(8,128)(2,1)S(1)} %fusion.18), kind=kOutput, calls=%fused_computation.34 | convolution fusion | flops 4718592 | bytes 4749312 | tf_op jit(solution)/shard_map/skcjb,scj->skb/dot_general | solution.py:56
  73.3 0.1 bitcast_select_fusion
  73.4 1.5 %scatter_custom_fusion.3 = f32[1024,128]{1,0:T(8,128)} fusion(s32[48]{0:T(128)S(1)} %fusion.23, f32[48,128]{1,0:T(8,128)S(1)} %reshape.209, f32[]{:T(128)} %constant.39.clone.1), kind=kCustom, calls=%fused_computation.11 | custom fusion | flops 6144 | bytes 524292 | tf_op jit(solution)/shard_map/scatter-add | solution.py:60
  74.9 0.0 reduce-scatter.2.cloned.1.call-update
  75.0 0.0 all-reduce.3.cloned.1.call-start
  75.0 19.6 %reduce-scatter.2.cloned.1.call-done = f32[256,128]{1,0:T(8,128)} async-done(((f32[1024,128]{1,0:T(8,128)}), f32[256,128]{1,0:T(8,128)}) %reduce-scatter.2.cloned.1.call-update) | async-done | bytes 131088 | tf_op jit(solution)/shard_map/reduce_scatter | solution.py:61
  94.6 0.0 all-reduce.3.cloned.1.call-update
  94.7 0.0 all-reduce.5.cloned.1.call-start
  94.7 18.4 %all-reduce.3.cloned.1.call-done = f32[256,128]{1,0:T(8,128)} async-done(((f32[256,128]{1,0:T(8,128)}), f32[256,128]{1,0:T(8,128)}) %all-reduce.3.cloned.1.call-update) | async-done | bytes 131088 | tf_op jit(solution)/shard_map/psum | solution.py:62
  113.1 0.0 all-reduce.5.cloned.1.call-update
  113.1 24.9 %all-reduce.5.cloned.1.call-done = f32[256,128]{1,0:T(8,128)} async-done(((f32[256,128]{1,0:T(8,128)}), f32[256,128]{1,0:T(8,128)}) %all-reduce.5.cloned.1.call-update) | async-done | bytes 131088 | tf_op jit(solution)/shard_map/psum | solution.py:62
  138.0 1.6 %copy.50 = f32[256,128]{1,0:T(8,128)} copy(f32[256,128]{1,0:T(8,128)} %all-reduce.5.cloned.1.call-done) | data formatting | bytes 262144
  (16 shorter events, 0.3 us)
Async XLA Ops:
  13.6 38.9 %all-to-all-start = ((s32[8,1,192]{2,1,0:T(1,128)}), s32[8,1,192]{2,1,0:T(1,128)S(1)}, u32[]{:S(2)}, u32[]{:S(2)}) async-start(s32[8,1,192]{2,1,0:T(1,128)} %all_to_all.9), calls=%async_computation | async-start | bytes 16384 | tf_op jit(solution)/shard_map/all_to_all | solution.py:31
  52.5 12.6 %all-to-all-start.1 = ((f32[8,6,192]{2,1,0:T(8,128)}), f32[8,6,192]{2,1,0:T(8,128)S(1)}, u32[]{:S(2)}, u32[]{:S(2)}) async-start(f32[8,6,192]{2,1,0:T(8,128)} %bitcast.8), calls=%async_computation.1 | async-start | bytes 131072 | tf_op jit(solution)/shard_map/all_to_all | solution.py:30
  58.2 36.4 %reduce-scatter.2.cloned.1.call-start = ((), (), s32[]{:S(2)}) async-start(), calls=%async_computation.3 | async-start | bytes 655360 | tf_op jit(solution)/shard_map/reduce_scatter | solution.py:61
  75.0 38.2 %all-reduce.3.cloned.1.call-start = ((), (), s32[]{:S(2)}) async-start(), calls=%async_computation.4 | async-start | bytes 262144 | tf_op jit(solution)/shard_map/psum | solution.py:62
  94.7 43.3 %all-reduce.5.cloned.1.call-start = ((), (), s32[]{:S(2)}) async-start(), calls=%async_computation.5 | async-start | bytes 262144 | tf_op jit(solution)/shard_map/psum | solution.py:62
Sparse Core Ops, SparseCore 0:
  75.1 19.5 reduce-scatter.1
  96.9 16.1 all-reduce.2
  115.4 22.5 all-reduce.4
